TPU v7x, 1024 devices: a whole 8x8x8 slice. The times are simulated.
1024 devices in a mesh: aux: 64 (over z, x), bas: 16 (over y, core).
Axes of the slice: x: 8, y: 8, z: 8, core: 2. Of those that a mesh axis runs over, the one named last changes fastest.
Arguments:
- three_centre: bfloat16 [16, 2, 64, 64, 8192], P('bas', None, None, None, 'aux'), may hold values from -0.25 to 0.25
- occ_green: bfloat16 [1024, 1024], P('bas'), may hold values from -0.5 to 0.5
- virt_blocks: bfloat16 [16, 64, 64], P('bas'), may hold values from -0.75 to 0.75
- row_lists: int32 [16, 2], P('bas'), may hold values from 0 to 15, as said below
Outputs:
- chi_band: float32 [8192, 2, 128], P('aux', None, 'bas')
Inputs may be any that keep to these rules, and one draw needn't show every extreme that they name: `row_lists`: each row holds 2 different block numbers; the first is the row's own block number.
All inputs are finite; a program needn't handle non-finite values.
Results may differ from a plain program's by a relative error of at most 0.004.
Values may be sent and summed in bfloat16 or wider, within the bound.
No kernel may reach another device: no remote copies, remote signals or barrier semaphores. Data moves between devices by JAX's collectives and lax.ppermute only.
A program may use at most 32 MiB of HBM per device.

v0:
```python
import jax
import jax.numpy as jnp
from jax import lax
from jax.sharding import PartitionSpec as P


def from_behind(block, axis, distance):
    devices = range(lax.axis_size(axis))
    route = [(i - distance, i) for i in devices if i - distance in devices]
    return lax.ppermute(block, axis, route)


def shards(three_centre, occ_green, virt_blocks, row_lists):
    mine = row_lists[0]
    kb = mine.shape[0]
    bb = virt_blocks.shape[1]
    slab = three_centre[0]
    aux_cols = slab.shape[-1]
    whole = lax.all_gather(occ_green, "bas", axis=0, tiled=True)
    nblk = whole.shape[0] // bb
    grid = whole.reshape(nblk, bb, nblk, bb)
    chosen = jnp.take(jnp.take(grid, mine, axis=0), mine, axis=2)
    matrix = chosen.reshape(kb * bb, kb * bb)
    half = jnp.dot(matrix, slab.reshape(kb * bb, bb * aux_cols), preferred_element_type=jnp.float32)
    half = half.astype(jnp.bfloat16).reshape(kb, bb, bb, aux_cols)
    full = jnp.einsum("kvlp,ls->kvsp", half, virt_blocks[0], preferred_element_type=jnp.float32)
    flat_full = full.astype(jnp.bfloat16).reshape(-1, aux_cols)
    flat_slab = slab.reshape(-1, aux_cols)
    contract = (((0,), (0,)), ((), ()))
    same = lax.dot_general(flat_full, flat_slab, contract, preferred_element_type=jnp.float32)
    following = from_behind(three_centre, "aux", -1)
    other = lax.dot_general(
        flat_full, following[0].reshape(-1, aux_cols), contract, preferred_element_type=jnp.float32
    )
    terms = jnp.stack([same, other], axis=1)
    summed = lax.psum_scatter(terms, "bas", scatter_dimension=2, tiled=True)
    return summed


def solution(mesh):
    in_specs = (
        P("bas", None, None, None, "aux"),
        P("bas", None),
        P("bas", None, None),
        P("bas", None),
    )
    out_specs = P("aux", None, "bas")
    return jax.shard_map(shards, mesh=mesh, in_specs=in_specs, out_specs=out_specs, check_vma=False)
```

profile of v0, /device:TPU:1, one launch (start us, length us, event | category | flops | bytes accessed | tf_op | source)
XLA Modules:
  0.0 210.8 jit_solution(7543526730594459831)
XLA Ops:
  6.5 0.7 all-gather.2.cloned.1.call-update
  7.3 0.0 all-reduce.3.cloned.1.call-start
  7.3 1.3 collective-permute-start
  8.6 0.7 fusion.11
  9.3 0.7 compare_and_fusion
  9.9 57.6 %all-gather.2.cloned.1.call-done = bf16[1024,1024]{1,0:T(8,128)(2,1)} async-done(((bf16[64,1024]{1,0:T(8,128)(2,1)}), bf16[1024,1024]{1,0:T(8,128)(2,1)}) %all-gather.2.cloned.1.call-update) | async-done | bytes 2097168 | tf_op jit(solution)/shard_map/all_gather | solution.py:19
  67.5 6.4 %reshape.76 = bf16[16,64,16,64]{3,2,1,0:T(8,128)(2,1)} reshape(bf16[1024,1024]{1,0:T(8,128)(2,1)} %all-gather.2.cloned.1.call-done) | data formatting | bytes 4194304 | tf_op jit(solution)/shard_map/reshape | solution.py:21
  73.9 3.0 %gather_fusion = bf16[2,64,16,64]{3,2,1,0:T(8,128)(2,1)S(1)} fusion(bf16[16,64,16,64]{3,2,1,0:T(8,128)(2,1)} %reshape.76, s32[1024]{0:T(1024)S(1)} %pad_clamp_fusion), kind=kCustom, calls=%fused_computation | custom fusion | bytes 524296 | tf_op jit(solution)/shard_map/jit(_take)/gather | solution.py:22
  76.8 0.1 broadcast_select_fusion
  77.0 0.1 copy.13
  77.1 0.6 gather_fusion.1
  77.7 0.1 select_bitcast_fusion
  77.8 0.1 copy.14
  77.8 0.1 select_n.40
  77.9 1.6 fusion.7
  79.6 0.6 copy.21
  80.2 0.8 fusion.4
  81.0 2.4 %convolution_bitcast_fusion = f32[128,1,128]{2,0,1:T(8,128)S(1)} fusion(bf16[8192,128]{1,0:T(8,128)(2,1)S(1)} %bitcast.45, bf16[8192,128]{1,0:T(8,128)(2,1)} %bitcast.11), kind=kOutput, calls=%fused_computation.9 | convolution fusion | flops 268435456 | bytes 4259840 | tf_op jit(solution)/shard_map/dot_general | solution.py:32
  83.4 0.8 convolution_bitcast_fusion.1
  84.2 0.8 copy.16
  85.0 1.3 dynamic-slice
  86.9 115.8 %all-reduce.3.cloned.1.call-done = f32[128,2,128]{0,1,2:T(2,128)} async-done(((f32[128,2,128]{0,1,2:T(2,128)}), f32[128,2,128]{0,1,2:T(2,128)}) %all-reduce.3.cloned.1.call-update) | async-done | bytes 131088
  202.7 0.7 constant_dynamic-slice_fusion
  203.4 0.6 copy.17
  (9 shorter events, 0.0 us)
Async XLA Ops:
  6.5 73.7 %copy-start = (bf16[1,64,64]{2,1,0:T(8,128)(2,1)S(1)}, bf16[1,64,64]{2,1,0:T(8,128)(2,1)}, u32[]{:S(2)}) copy-start(bf16[1,64,64]{2,1,0:T(8,128)(2,1)} %param.6) | copy-start | bytes 24580
  6.5 60.9 %all-gather.2.cloned.1.call-start = ((), (), s32[]{:S(2)}) async-start(), calls=%async_computation | async-start | bytes 2228224 | tf_op jit(solution)/shard_map/all_gather | solution.py:19
  7.3 195.4 %all-reduce.3.cloned.1.call-start = ((), (), s32[]{:S(2)}) async-start(), calls=%async_computation.1 | async-start | bytes 262144
  7.3 73.7 %collective-permute-start = (bf16[1,2,64,64,128]{4,3,2,1,0:T(8,128)(2,1)}, bf16[1,2,64,64,128]{4,3,2,1,0:T(8,128)(2,1)}, u32[]{:S(2)}, u32[]{:S(2)}) collective-permute-start(bf16[1,2,64,64,128]{4,3,2,1,0:T(8,128)(2,1)} %param.4), channel_id=1, source_target_pairs={{16,0},{32,16},{48,32},{64,48},{80,64},{96,80},{112,96},{128,112},... | collective-permute-start | bytes 6291464 | tf_op jit(solution)/shard_map/ppermute | solution.py:10
  73.9 4.1 %copy-start.1 = (bf16[1,2,64,64,128]{4,3,2,1,0:T(8,128)(2,1)S(1)}, bf16[1,2,64,64,128]{4,3,2,1,0:T(8,128)(2,1)}, u32[]{:S(2)}) copy-start(bf16[1,2,64,64,128]{4,3,2,1,0:T(8,128)(2,1)} %param.4) | copy-start | bytes 6291460
Sparse Core Ops, SparseCore 0:
  10.1 57.3 all-gather.1
  85.1 117.5 all-reduce.2
where the time goes:
time: 211 us
  waiting for transfers between devices  174 us (82%)
  local copies, waits for them, and re-layouts  14.2 us (7%)
  between operations  14.2 us (7%)
  matrix products  5.58 us (3%)
    unnamed x3, waiting for transfers between devices  117 us
    all_gather x1, waiting for transfers between devices, shards(): whole = lax.all_gather(occ_green, 'bas', axis=0, tiled=True)  57.6 us
    reshape x1, local copies, waits for them, and re-layouts, shards(): grid = whole.reshape(nblk, bb, nblk, bb)  6.37 us
  transfers between devices with their start and end apart: 3, of which 2 were waited for; matrix products, arithmetic and copies ran while one was open for 8% of the time, Pallas kernels for 0%

commit v1 on v0

v1 whole, which is shorter than its diff:
```python
import jax
import jax.numpy as jnp
from jax import lax
from jax.sharding import PartitionSpec as P


def shards(three_centre, occ_green, virt_blocks, row_lists):
    n_aux, n_bas = lax.axis_size("aux"), lax.axis_size("bas")
    me = lax.axis_index("bas")
    odd = lax.rem(me, 2) == 1
    first = jnp.logical_and(me == 0, lax.axis_index("aux") == 0)
    both = ("aux", "bas")
    bb = virt_blocks.shape[1]
    slab = three_centre[0]
    kb, aux_cols = slab.shape[0], slab.shape[-1]
    other_block = row_lists[0, 1]

    def at(a, c):
        return a * n_bas + c

    route = []
    for a in range(n_aux - 1):
        for c in range(n_bas):
            if c % 2 == 1:
                route.append((at(a, c), at(a + 1, c)))
            elif (a, c) == (0, 0):
                route.append((at(1, 0), at(0, 1)))
            else:
                route.append((at(a + 1, c), at(a, c)))
    arrived = lax.ppermute(slab, both, route)
    handed = lax.ppermute(arrived, both, [(at(0, 1), at(0, 0))])

    rows = occ_green.reshape(bb, n_bas, bb).transpose(1, 0, 2)
    own = lax.dynamic_index_in_dim(rows, me, 0, keepdims=False)
    beside = lax.dynamic_index_in_dim(rows, other_block, 0, keepdims=False)
    sent = jnp.stack([rows, jnp.broadcast_to(own, rows.shape)], axis=1)
    got = lax.all_to_all(sent, "bas", 0, 0)
    there = lax.dynamic_index_in_dim(got, other_block, 0, keepdims=False)
    matrix = jnp.concatenate(
        [jnp.concatenate([own, beside], axis=1), jnp.concatenate([there[0], there[1]], axis=1)], axis=0
    )
    virt = virt_blocks[0]
    matrix = jnp.where(odd, matrix.T, matrix)
    virt = jnp.where(odd, virt.T, virt)

    half = jnp.dot(matrix, slab.reshape(kb * bb, bb * aux_cols), preferred_element_type=jnp.float32)
    half = half.astype(jnp.bfloat16).reshape(kb, bb, bb, aux_cols)
    full = jnp.einsum("kvlp,ls->kvsp", half, virt, preferred_element_type=jnp.float32)
    flat_full = full.astype(jnp.bfloat16).reshape(-1, aux_cols)

    def tile(block):
        contract = (((0,), (0,)), ((), ()))
        product = lax.dot_general(
            block.reshape(-1, aux_cols), flat_full, contract, preferred_element_type=jnp.float32
        )
        return jnp.where(odd, product.T, product)

    same = tile(slab)
    pair = tile(jnp.where(first, handed, arrived))
    back = [(at(a + 1, c), at(a, c)) for a in range(n_aux - 1) for c in range(1, n_bas, 2)]
    returned = lax.ppermute(pair, both, back)
    ahead = jnp.where(odd, returned, pair)

    cut = aux_cols // n_bas
    parts = jnp.stack([same.reshape(n_bas, cut, aux_cols), ahead.reshape(n_bas, cut, aux_cols)], axis=1)
    total = lax.all_to_all(parts, "bas", 0, 0).sum(axis=0)
    return total.transpose(2, 0, 1)


def solution(mesh):
    in_specs = (
        P("bas", None, None, None, "aux"),
        P("bas", None),
        P("bas", None, None),
        P("bas", None),
    )
    out_specs = P("aux", None, "bas")
    return jax.shard_map(shards, mesh=mesh, in_specs=in_specs, out_specs=out_specs, check_vma=False)
```

time: 211 us -> 89.7 us (0.43)
  the two profiles are of different devices: /device:TPU:1 before, /device:TPU:399 now
where the time goes in v1:
time: 89.7 us; the launch traced here: 89.3 us
  waiting for transfers between devices  41.3 us (46%)
  starting transfers between devices  20.5 us (23%)
  blocking collectives  11.6 us (13%)
  matrix products  6.42 us (7%)
  local copies, waits for them, and re-layouts  6.33 us (7%)
  between operations  2.31 us (3%)
    ppermute x1, waiting for transfers between devices, shards(): arrived = lax.ppermute(slab, both, route)  23.3 us
    all_to_all x1, waiting for transfers between devices, shards(): got = lax.all_to_all(sent, 'bas', 0, 0)  11.6 us
    all_to_all x1, blocking collectives, shards(): total = lax.all_to_all(parts, 'bas', 0, 0).sum(axis=0)  11.6 us
    all_to_all x1, starting transfers between devices, shards(): got = lax.all_to_all(sent, 'bas', 0, 0)  10.6 us
    ppermute x1, waiting for transfers between devices, shards(): returned = lax.ppermute(pair, both, back)  6.38 us
    ppermute x1, starting transfers between devices, shards(): arrived = lax.ppermute(slab, both, route)  6.04 us
    dot_general x2, matrix products, tile(): lax.dot_general(block.reshape(-1, aux_cols), flat_full, contract, preferr...  4.01 us
    unnamed x10, local copies, waits for them, and re-layouts  3.39 us
  transfers between devices with their start and end apart: 4, of which 3 were waited for; matrix products, arithmetic and copies ran while one was open for 9% of the time, Pallas kernels for 0%

profile of v1, /device:TPU:399, one launch (start us, length us, event | category | flops | bytes accessed | tf_op | source)
XLA Modules:
  0.0 89.3 jit_solution(14294364406759787356)
XLA Ops:
  0.0 6.0 %collective-permute-start = (bf16[2,64,64,128]{3,2,1,0:T(8,128)(2,1)}, bf16[2,64,64,128]{3,2,1,0:T(8,128)(2,1)}, u32[]{:S(2)}, u32[]{:S(2)}) collective-permute-start(bf16[2,64,64,128]{3,2,1,0:T(8,128)(2,1)} %bitcast.76), channel_id=1, source_target_pairs={{16,1},{1,17},{18,2},{3,19},{20,4},{5,21},{22,6},{7,23},{24,8},{9,... | collective-permute-start | bytes 6291464 | tf_op jit(solution)/shard_map/ppermute | solution.py:30
  6.1 23.3 %collective-permute-done = bf16[2,64,64,128]{3,2,1,0:T(8,128)(2,1)} collective-permute-done((bf16[2,64,64,128]{3,2,1,0:T(8,128)(2,1)}, bf16[2,64,64,128]{3,2,1,0:T(8,128)(2,1)}, u32[]{:S(2)}, u32[]{:S(2)}) %collective-permute-start) | collective-permute-done | bytes 2097184 | tf_op jit(solution)/shard_map/ppermute | solution.py:30
  29.3 2.0 %collective-permute-start.1 = (bf16[2,64,64,128]{3,2,1,0:T(8,128)(2,1)}, bf16[2,64,64,128]{3,2,1,0:T(8,128)(2,1)}, u32[]{:S(2)}, u32[]{:S(2)}) collective-permute-start(bf16[2,64,64,128]{3,2,1,0:T(8,128)(2,1)} %collective-permute-done), channel_id=1, source_target_pairs={{1,0}} | collective-permute-start | bytes 6291464 | tf_op jit(solution)/shard_map/ppermute | solution.py:31
  31.3 1.2 %slice.11 = s32[1,1]{1,0:T(1,128)} slice(s32[1,2]{1,0:T(1,128)} %param.7), slice={[0:1], [1:2]} | slice | bytes 8 | tf_op jit(solution)/shard_map/slice | solution.py:16
  33.8 1.1 %reshape.18 = bf16[64,16,64]{2,1,0:T(8,128)(2,1)S(1)} reshape(bf16[64,1024]{1,0:T(8,128)(2,1)} %param.5) | data formatting | bytes 262144 | tf_op jit(solution)/shard_map/reshape | solution.py:33
  36.0 0.1 pad_maximum_fusion
  36.1 1.1 %reshape.23 = bf16[16,2,4096]{2,1,0:T(2,128)(2,1)} reshape(bf16[16,2,64,64]{3,2,1,0:T(8,128)(2,1)S(1)} %pad_maximum_fusion) | data formatting | bytes 524288
  37.2 10.6 %all-to-all-start = ((bf16[16,2,4096]{2,1,0:T(2,128)(2,1)}), bf16[16,2,4096]{2,1,0:T(2,128)(2,1)S(1)}, u32[]{:S(2)}, u32[]{:S(2)}) async-start(bf16[16,2,4096]{2,1,0:T(2,128)(2,1)} %reshape.23), calls=%async_computation | async-start | bytes 524288 | tf_op jit(solution)/shard_map/all_to_all | solution.py:37
  47.8 0.1 copy.22
  47.9 11.6 %all-to-all-done = bf16[16,2,4096]{2,1,0:T(2,128)(2,1)S(1)} async-done(((bf16[16,2,4096]{2,1,0:T(2,128)(2,1)}), bf16[16,2,4096]{2,1,0:T(2,128)(2,1)S(1)}, u32[]{:S(2)}, u32[]{:S(2)}) %all-to-all-start) | async-done | bytes 262176 | tf_op jit(solution)/shard_map/all_to_all | solution.py:37
  59.5 0.3 reshape.24
  60.0 0.1 copy.24
  60.1 1.6 %fusion.11 = bf16[16,8,64,128]{3,1,2,0:T(8,128)(2,1)S(1)} fusion(bf16[16,8,64,128]{3,2,1,0:T(8,128)(2,1)S(1)} %bitcast.77, bf16[128,128]{1,0:T(8,128)(2,1)S(1)} %copy.24, pred[]{:T(512)S(6)} %eq.9, bf16[64,64]{1,0:T(8,128)(2,1)S(1)} %get-tuple-element.6, bf16[64,64]{1,0:T(8,128)(2,1)S(1)} %get-tuple-element.5, bf16[64,64]{1,0:T(8,128)(2,1)S(1)} %get-tuple-element.9, ...), kind=kOutput, calls=%fused_computation.10 | convolution fusion | flops 269631488 | bytes 4259841 | tf_op jit(solution)/shard_map/dot_general | solution.py:46
  61.8 0.6 copy.36
  62.4 0.8 fusion.8
  63.2 1.3 %copy-done.1 = bf16[64,2,64,128]{3,0,2,1:T(8,128)(2,1)} copy-done((bf16[64,2,64,128]{3,0,2,1:T(8,128)(2,1)}, bf16[64,2,64,128]{3,0,2,1:T(8,128)(2,1)S(1)}, u32[]{:S(2)}) %copy-start.1) | copy-done | bytes 2097176
  64.5 0.8 fusion.26
  65.3 0.1 copy.26
  65.4 3.2 %fusion.14 = f32[128,128]{1,0:T(8,128)S(1)} fusion(bf16[64,2,64,128]{3,0,2,1:T(8,128)(2,1)} %copy-done.1, bf16[2,64,64,128]{3,2,1,0:T(8,128)(2,1)} %collective-permute-done.1, bf16[2,64,64,128]{3,2,1,0:T(8,128)(2,1)} %collective-permute-done, pred[]{:T(512)S(6)} %and.6), kind=kOutput, calls=%fused_computation.11 | convolution fusion | flops 269484032 | bytes 6356993 | tf_op jit(solution)/shard_map/dot_general | solution.py:53
  68.6 0.1 copy.27
  68.7 1.9 %collective-permute-start.2 = (f32[128,128]{1,0:T(8,128)S(1)}, f32[128,128]{1,0:T(8,128)S(1)}, u32[]{:S(2)}, u32[]{:S(2)}) collective-permute-start(f32[128,128]{1,0:T(8,128)S(1)} %bitcast_select_fusion), channel_id=1, source_target_pairs={{17,1},{19,3},{21,5},{23,7},{25,9},{27,11},{29,13},{31,15},{33,17}... | collective-permute-start | bytes 196616 | tf_op jit(solution)/shard_map/ppermute | solution.py:61
  70.7 6.4 %collective-permute-done.2 = f32[128,128]{1,0:T(8,128)S(1)} collective-permute-done((f32[128,128]{1,0:T(8,128)S(1)}, f32[128,128]{1,0:T(8,128)S(1)}, u32[]{:S(2)}, u32[]{:S(2)}) %collective-permute-start.2) | collective-permute-done | bytes 65568 | tf_op jit(solution)/shard_map/ppermute | solution.py:61
  77.1 11.6 %all_to_all.10 = f32[16,2,8,128]{3,2,1,0:T(8,128)S(1)} all-to-all(f32[16,2,8,128]{3,2,1,0:T(8,128)S(1)} %pad_maximum_fusion.1), channel_id=1, replica_groups=mesh['aux'=64,'bas'=16] {'bas'}, dimensions={0} | all-to-all | bytes 262144 | tf_op jit(solution)/shard_map/all_to_all | solution.py:66
  88.7 0.6 reduce_sum.9
  (16 shorter events, 0.4 us)
Async XLA Ops:
  0.0 47.8 %copy-start.2 = (bf16[1,64,64]{2,1,0:T(8,128)(2,1)S(1)}, bf16[1,64,64]{2,1,0:T(8,128)(2,1)}, u32[]{:S(2)}) copy-start(bf16[1,64,64]{2,1,0:T(8,128)(2,1)} %param.6) | copy-start | bytes 24580
  0.0 29.3 %collective-permute-start = (bf16[2,64,64,128]{3,2,1,0:T(8,128)(2,1)}, bf16[2,64,64,128]{3,2,1,0:T(8,128)(2,1)}, u32[]{:S(2)}, u32[]{:S(2)}) collective-permute-start(bf16[2,64,64,128]{3,2,1,0:T(8,128)(2,1)} %bitcast.76), channel_id=1, source_target_pairs={{16,1},{1,17},{18,2},{3,19},{20,4},{5,21},{22,6},{7,23},{24,8},{9,... | collective-permute-start | bytes 6291464 | tf_op jit(solution)/shard_map/ppermute | solution.py:30
  29.3 36.0 %collective-permute-start.1 = (bf16[2,64,64,128]{3,2,1,0:T(8,128)(2,1)}, bf16[2,64,64,128]{3,2,1,0:T(8,128)(2,1)}, u32[]{:S(2)}, u32[]{:S(2)}) collective-permute-start(bf16[2,64,64,128]{3,2,1,0:T(8,128)(2,1)} %collective-permute-done), channel_id=1, source_target_pairs={{1,0}} | collective-permute-start | bytes 6291464 | tf_op jit(solution)/shard_map/ppermute | solution.py:31
  35.0 25.1 %copy-start = (bf16[1,2,64,64,128]{4,3,2,1,0:T(8,128)(2,1)S(1)}, bf16[1,2,64,64,128]{4,3,2,1,0:T(8,128)(2,1)}, u32[]{:S(2)}) copy-start(bf16[1,2,64,64,128]{4,3,2,1,0:T(8,128)(2,1)} %param.4) | copy-start | bytes 6291460
  37.2 22.3 %all-to-all-start = ((bf16[16,2,4096]{2,1,0:T(2,128)(2,1)}), bf16[16,2,4096]{2,1,0:T(2,128)(2,1)S(1)}, u32[]{:S(2)}, u32[]{:S(2)}) async-start(bf16[16,2,4096]{2,1,0:T(2,128)(2,1)} %reshape.23), calls=%async_computation | async-start | bytes 524288 | tf_op jit(solution)/shard_map/all_to_all | solution.py:37
  63.2 1.3 %copy-start.1 = (bf16[64,2,64,128]{3,0,2,1:T(8,128)(2,1)}, bf16[64,2,64,128]{3,0,2,1:T(8,128)(2,1)S(1)}, u32[]{:S(2)}) copy-start(bf16[64,2,64,128]{3,0,2,1:T(8,128)(2,1)S(1)} %fusion.8) | copy-start | bytes 6291460
  68.7 8.3 %collective-permute-start.2 = (f32[128,128]{1,0:T(8,128)S(1)}, f32[128,128]{1,0:T(8,128)S(1)}, u32[]{:S(2)}, u32[]{:S(2)}) collective-permute-start(f32[128,128]{1,0:T(8,128)S(1)} %bitcast_select_fusion), channel_id=1, source_target_pairs={{17,1},{19,3},{21,5},{23,7},{25,9},{27,11},{29,13},{31,15},{33,17}... | collective-permute-start | bytes 196616 | tf_op jit(solution)/shard_map/ppermute | solution.py:61

commit v2 on v1

v2 whole, which is shorter than its diff:
```python
import jax
import jax.numpy as jnp
from jax import lax
from jax.experimental import pallas as pl
from jax.experimental.pallas import tpu as pltpu
from jax.sharding import PartitionSpec as P

VMEM = pl.BlockSpec(memory_space=pltpu.VMEM)
SMEM = pl.BlockSpec(memory_space=pltpu.SMEM)
ANY = pl.BlockSpec(memory_space=pl.ANY)
LIMIT = 24 * 2**20
PIECES = 4
GROUP = 4
STRIP = 16


def is_odd():
    return lax.rem(lax.axis_index("bas"), 2) == 1


def is_first():
    return jnp.logical_and(lax.axis_index("bas") == 0, lax.axis_index("aux") == 0)


def blocks_kernel(lists, occ, virt, slab, sent, upper, spread, held, sem):
    fetch = pltpu.make_async_copy(slab, held, sem)
    fetch.start()
    rows, width = occ.shape[0], 2 * occ.shape[0]
    low_lanes = lax.broadcasted_iota(jnp.int32, (rows, width), 1) < rows

    def in_high_lanes(number):
        tile = occ[:, pl.ds(pl.multiple_of(number // 2 * width, width), width)].astype(jnp.float32)
        return jnp.where(lax.rem(number, 2) == 1, tile, pltpu.roll(tile, rows, 1))

    own = in_high_lanes(lax.axis_index("bas"))
    upper[...] = jnp.where(low_lanes, pltpu.roll(own, rows, 1), in_high_lanes(lists[0, 1])).astype(upper.dtype)
    for t in range(occ.shape[1] // width):
        tile = occ[:, t * width : (t + 1) * width].astype(jnp.float32)
        sent[2 * t] = jnp.where(low_lanes, tile, own).astype(sent.dtype)
        sent[2 * t + 1] = jnp.where(low_lanes, pltpu.roll(tile, rows, 1), own).astype(sent.dtype)
    v = virt[0].astype(jnp.float32)
    v = jnp.where(is_odd(), v, v.T)
    zero = jnp.zeros_like(v)
    strips = [jnp.concatenate([v if i == j else zero for j in range(GROUP)], axis=1) for i in range(GROUP)]
    spread[...] = jnp.concatenate(strips, axis=0).astype(spread.dtype)
    fetch.wait()


def blocks_of(lists, occ, virt, slab):
    rows, cols = occ.shape
    return pl.pallas_call(
        blocks_kernel,
        out_shape=[
            jax.ShapeDtypeStruct((cols // rows, rows, 2 * rows), occ.dtype),
            jax.ShapeDtypeStruct((rows, 2 * rows), occ.dtype),
            jax.ShapeDtypeStruct((GROUP * rows, GROUP * rows), virt.dtype),
            jax.ShapeDtypeStruct(slab.shape, slab.dtype),
        ],
        in_specs=[SMEM, VMEM, VMEM, ANY],
        out_specs=[VMEM] * 4,
        scratch_shapes=[pltpu.SemaphoreType.DMA],
        compiler_params=pltpu.CompilerParams(vmem_limit_bytes=LIMIT),
    )(lists, occ, virt, slab)


def transform_kernel(lists, upper, got, spread, slab, left, same, halves):
    n_rows, bb, cols = slab.shape
    matrix = jnp.concatenate([upper[...], got[lists[0, 1]]], axis=0).astype(jnp.float32)
    matrix = jnp.where(is_odd(), matrix.T, matrix).astype(jnp.bfloat16)
    for r in range(0, bb, STRIP):
        turned = jnp.swapaxes(slab[:, r : r + STRIP, :], 0, 1)
        parts = []
        for q in range(0, STRIP, 2):
            two = jnp.concatenate([turned[q], turned[q + 1]], axis=1)
            half = jnp.dot(matrix, two, preferred_element_type=jnp.float32).astype(jnp.bfloat16)
            parts += [half[:, :cols], half[:, cols:]]
        halves[:, r : r + STRIP, :] = jnp.swapaxes(jnp.stack(parts), 0, 1)
    for g in range(0, n_rows, GROUP):
        half = halves[g : g + GROUP].reshape(GROUP * bb, cols)
        full = jnp.dot(spread[...], half, preferred_element_type=jnp.float32)
        left[:, g * bb : (g + GROUP) * bb] = full.T.astype(jnp.bfloat16)
    store_product(same, left, slab.reshape(n_rows * bb, cols))


def store_product(out, left, right):
    depth = left.shape[1]
    step = depth // PIECES
    total = jnp.zeros(out.shape, jnp.float32)
    for i in range(0, depth, step):
        total += jnp.dot(left[:, i : i + step], right[i : i + step], preferred_element_type=jnp.float32)
    out[...] = jnp.where(is_odd(), total, total.T)


def transform(lists, upper, got, spread, slab):
    n_rows, bb, cols = slab.shape
    return pl.pallas_call(
        transform_kernel,
        out_shape=[
            jax.ShapeDtypeStruct((cols, n_rows * bb), jnp.bfloat16),
            jax.ShapeDtypeStruct((cols, cols), jnp.float32),
        ],
        in_specs=[SMEM] + [VMEM] * 4,
        out_specs=[VMEM, VMEM],
        scratch_shapes=[pltpu.VMEM(slab.shape, slab.dtype)],
        compiler_params=pltpu.CompilerParams(vmem_limit_bytes=LIMIT),
    )(lists, upper, got, spread, slab)


def pair_kernel(left, arrived, handed, out, block, sem):
    @pl.when(is_first())
    def _():
        copy = pltpu.make_async_copy(handed, block, sem)
        copy.start()
        copy.wait()
        store_product(out, left, block)

    @pl.when(jnp.logical_not(is_first()))
    def _():
        store_product(out, left, arrived)


def pair_product(left, arrived, handed):
    cols = arrived.shape[1]
    return pl.pallas_call(
        pair_kernel,
        out_shape=jax.ShapeDtypeStruct((cols, cols), jnp.float32),
        in_specs=[VMEM, VMEM, ANY],
        out_specs=VMEM,
        scratch_shapes=[pltpu.VMEM(arrived.shape, arrived.dtype), pltpu.SemaphoreType.DMA],
        compiler_params=pltpu.CompilerParams(vmem_limit_bytes=LIMIT),
    )(left, arrived, handed)


def shards(three_centre, occ_green, virt_blocks, row_lists):
    n_aux, n_bas = lax.axis_size("aux"), lax.axis_size("bas")
    both = ("aux", "bas")
    bb = virt_blocks.shape[1]
    slab = three_centre[0]
    kb, aux_cols = slab.shape[0], slab.shape[-1]

    def at(a, c):
        return a * n_bas + c

    route = []
    for a in range(n_aux - 1):
        for c in range(n_bas):
            if c % 2 == 1:
                route.append((at(a, c), at(a + 1, c)))
            elif (a, c) == (0, 0):
                route.append((at(1, 0), at(0, 1)))
            else:
                route.append((at(a + 1, c), at(a, c)))
    arrived = lax.ppermute(slab, both, route)

    sent, upper, spread, held = blocks_of(row_lists, occ_green, virt_blocks, slab.reshape(kb * bb, bb, aux_cols))
    got = lax.all_to_all(sent, "bas", 0, 0)
    left, same = transform(row_lists, upper, got, spread, held)

    arrived, left, same = lax.optimization_barrier((arrived, left, same))
    handed = lax.ppermute(arrived, both, [(at(0, 1), at(0, 0))])
    pair = pair_product(left, arrived.reshape(-1, aux_cols), handed.reshape(-1, aux_cols))
    back = [(at(a + 1, c), at(a, c)) for a in range(n_aux - 1) for c in range(1, n_bas, 2)]
    returned = lax.ppermute(pair, both, back)
    ahead = jnp.where(is_odd(), returned, pair)

    cut = aux_cols // n_bas
    parts = jnp.stack([same.reshape(n_bas, cut, aux_cols), ahead.reshape(n_bas, cut, aux_cols)], axis=1)
    total = lax.all_to_all(parts, "bas", 0, 0).sum(axis=0)
    return total.transpose(2, 0, 1)


def solution(mesh):
    in_specs = (
        P("bas", None, None, None, "aux"),
        P("bas", None),
        P("bas", None, None),
        P("bas", None),
    )
    out_specs = P("aux", None, "bas")
    return jax.shard_map(shards, mesh=mesh, in_specs=in_specs, out_specs=out_specs, check_vma=False)
```

time: 89.7 us -> 60.4 us (0.67)
  the two profiles are of different devices: /device:TPU:399 before, /device:TPU:1 now
where the time goes in v2:
time: 60.4 us; the launch traced here: 60.1 us
  blocking collectives  35.8 us (59%)
  waiting for transfers between devices  7.34 us (12%)
  starting transfers between devices  6.65 us (11%)
  Pallas kernels  5.76 us (10%)
  local copies, waits for them, and re-layouts  3.87 us (6%)
  other arithmetic  0.64 us (1%)
    all_to_all x1, blocking collectives, shards(): got = lax.all_to_all(sent, 'bas', 0, 0)  25.3 us
    all_to_all x1, blocking collectives, shards(): total = lax.all_to_all(parts, 'bas', 0, 0).sum(axis=0)  10.5 us
    pallas_call x1, Pallas kernels, transform(): pl.pallas_call(transform_kernel, out_shape=[jax.ShapeDtypeStruct((cols, n...  4.08 us
    ppermute x1, starting transfers between devices, shards(): arrived = lax.ppermute(slab, both, route)  3.94 us
    unnamed x8, local copies, waits for them, and re-layouts  3.87 us
    ppermute x1, waiting for transfers between devices, shards(): returned = lax.ppermute(pair, both, back)  3.71 us
    ppermute x1, waiting for transfers between devices, shards(): handed = lax.ppermute(arrived, both, [(at(0, 1), at(0, 0))])  3.63 us
    ppermute x1, starting transfers between devices, shards(): handed = lax.ppermute(arrived, both, [(at(0, 1), at(0, 0))])  1.42 us
  transfers between devices with their start and end apart: 3, of which 2 were waited for; matrix products, arithmetic and copies ran while one was open for 0% of the time, Pallas kernels for 8%

profile of v2, /device:TPU:1, one launch (start us, length us, event | category | flops | bytes accessed | tf_op | source)
XLA Modules:
  0.0 60.1 jit_solution(17731936511256749075)
XLA Ops:
  0.0 3.9 %collective-permute-start = (bf16[2,64,64,128]{3,2,1,0:T(8,128)(2,1)}, bf16[2,64,64,128]{3,2,1,0:T(8,128)(2,1)S(1)}, u32[]{:S(2)}, u32[]{:S(2)}) collective-permute-start(bf16[2,64,64,128]{3,2,1,0:T(8,128)(2,1)} %bitcast.14), channel_id=1, source_target_pairs={{16,1},{1,17},{18,2},{3,19},{20,4},{5,21},{22,6},{7,23},{24,8},{9,... | collective-permute-start | bytes 6291464 | tf_op jit(solution)/shard_map/ppermute | solution.py:153
  3.9 0.0 copy-start
  4.0 1.6 %copy-done = bf16[1,2,64,64,128]{4,3,2,1,0:T(8,128)(2,1)S(1)} copy-done((bf16[1,2,64,64,128]{4,3,2,1,0:T(8,128)(2,1)S(1)}, bf16[1,2,64,64,128]{4,3,2,1,0:T(8,128)(2,1)}, u32[]{:S(2)}) %copy-start) | copy-done | bytes 2097176
  5.5 0.0 copy-start.1
  5.5 0.9 %copy-done.1 = bf16[64,1024]{1,0:T(8,128)(2,1)S(1)} copy-done((bf16[64,1024]{1,0:T(8,128)(2,1)S(1)}, bf16[64,1024]{1,0:T(8,128)(2,1)}, u32[]{:S(2)}) %copy-start.1) | copy-done | bytes 131096
  6.5 0.0 copy-start.2
  6.5 0.7 %copy-done.2 = bf16[1,64,64]{2,1,0:T(8,128)(2,1)S(1)} copy-done((bf16[1,64,64]{2,1,0:T(8,128)(2,1)S(1)}, bf16[1,64,64]{2,1,0:T(8,128)(2,1)}, u32[]{:S(2)}) %copy-start.2) | copy-done | bytes 8216
  7.2 0.0 copy-start.3
  7.2 0.7 %copy-done.3 = s32[1,2]{1,0:T(1,128)S(1)} copy-done((s32[1,2]{1,0:T(1,128)S(1)}, s32[1,2]{1,0:T(1,128)}, u32[]{:S(2)}) %copy-start.3) | copy-done | bytes 32
  7.8 0.9 %shard_map.46 = (bf16[16,64,128]{2,1,0:T(8,128)(2,1)S(1)}, bf16[64,128]{1,0:T(8,128)(2,1)S(1)}, bf16[256,256]{1,0:T(8,128)(2,1)S(1)}, bf16[128,64,128]{2,1,0:T(8,128)(2,1)S(1)}) custom-call(s32[1,2]{1,0:T(1,128)S(1)} %copy-done.3, bf16[64,1024]{1,0:T(8,128)(2,1)S(1)} %copy-done.1, bf16[1,64,64]{2,1,0:T(8,128)(2,1)S(1)} %copy-done.2, ...), custom_call_target="tpu_custom_call" | custom-call | tf_op jit(solution)/shard_map/pallas_call | solution.py:51
  8.7 25.3 %all_to_all.10.got = bf16[16,64,128]{2,1,0:T(8,128)(2,1)S(1)} all-to-all(bf16[16,64,128]{2,1,0:T(8,128)(2,1)S(1)} %get-tuple-element.15), channel_id=1, replica_groups=mesh['aux'=64,'bas'=16] {'bas'}, dimensions={0} | all-to-all | bytes 524288 | tf_op jit(solution)/shard_map/all_to_all | solution.py:156
  34.0 4.1 %shard_map.47 = (bf16[128,8192]{1,0:T(8,128)(2,1)S(1)}, f32[128,128]{1,0:T(8,128)S(1)}) custom-call(s32[1,2]{1,0:T(1,128)S(1)} %copy-done.3, bf16[64,128]{1,0:T(8,128)(2,1)S(1)} %get-tuple-element.14.upper, bf16[16,64,128]{2,1,0:T(8,128)(2,1)S(1)} %all_to_all.10.got, bf16[256,256]{1,0:T(8,128)(2,1)S(1)} %get-tuple-element.16.spread, ...), custom_call_target="tpu_custom_call" | custom-call | tf_op jit(solution)/shard_map/pallas_call | solution.py:96
  38.1 0.0 collective-permute-done
  38.1 1.4 %collective-permute-start.1 = (bf16[2,64,64,128]{3,2,1,0:T(8,128)(2,1)S(1)}, bf16[2,64,64,128]{3,2,1,0:T(8,128)(2,1)S(1)}, u32[]{:S(2)}, u32[]{:S(2)}) collective-permute-start(bf16[2,64,64,128]{3,2,1,0:T(8,128)(2,1)S(1)} %collective-permute-done), channel_id=1, source_target_pairs={{1,0}} | collective-permute-start | bytes 6291464 | tf_op jit(solution)/shard_map/ppermute | solution.py:160
  39.5 3.6 %collective-permute-done.1 = bf16[2,64,64,128]{3,2,1,0:T(8,128)(2,1)S(1)} collective-permute-done((bf16[2,64,64,128]{3,2,1,0:T(8,128)(2,1)S(1)}, bf16[2,64,64,128]{3,2,1,0:T(8,128)(2,1)S(1)}, u32[]{:S(2)}, u32[]{:S(2)}) %collective-permute-start.1) | collective-permute-done | bytes 2097184 | tf_op jit(solution)/shard_map/ppermute | solution.py:160
  43.2 0.8 %shard_map.48 = f32[128,128]{1,0:T(8,128)S(1)} custom-call(bf16[128,8192]{1,0:T(8,128)(2,1)S(1)} %get-tuple-element.21.left, bf16[8192,128]{1,0:T(8,128)(2,1)S(1)} %bitcast.12, bf16[8192,128]{1,0:T(8,128)(2,1)S(1)} %bitcast.13), custom_call_target="tpu_custom_call" | custom-call | tf_op jit(solution)/shard_map/pallas_call | solution.py:124
  44.0 1.3 %collective-permute-start.2 = (f32[128,128]{1,0:T(8,128)S(1)}, f32[128,128]{1,0:T(8,128)S(1)}, u32[]{:S(2)}, u32[]{:S(2)}) collective-permute-start(f32[128,128]{1,0:T(8,128)S(1)} %shard_map.48), channel_id=1, source_target_pairs={{17,1},{19,3},{21,5},{23,7},{25,9},{27,11},{29,13},{31,15},{33,17}... | collective-permute-start | bytes 196616 | tf_op jit(solution)/shard_map/ppermute | solution.py:163
  45.3 3.7 %collective-permute-done.2 = f32[128,128]{1,0:T(8,128)S(1)} collective-permute-done((f32[128,128]{1,0:T(8,128)S(1)}, f32[128,128]{1,0:T(8,128)S(1)}, u32[]{:S(2)}, u32[]{:S(2)}) %collective-permute-start.2) | collective-permute-done | bytes 65568 | tf_op jit(solution)/shard_map/ppermute | solution.py:163
  49.0 10.5 %all_to_all.11 = f32[16,2,8,128]{3,2,1,0:T(8,128)S(1)} all-to-all(f32[16,2,8,128]{3,2,1,0:T(8,128)S(1)} %pad_maximum_fusion), channel_id=1, replica_groups=mesh['aux'=64,'bas'=16] {'bas'}, dimensions={0} | all-to-all | bytes 262144 | tf_op jit(solution)/shard_map/all_to_all | solution.py:168
  59.5 0.6 %reduce_sum.9 = f32[2,8,128]{2,1,0:T(8,128)} reduce(f32[16,2,8,128]{3,2,1,0:T(8,128)S(1)} %all_to_all.11, f32[]{:T(128)} %constant.11.clone.1), dimensions={0}, to_apply=%region_0.1 | reduce | flops 30720 | bytes 139268 | tf_op jit(solution)/shard_map/reduce_sum | solution.py:168
  (2 shorter events, 0.0 us)
Async XLA Ops:
  0.0 38.1 %collective-permute-start = (bf16[2,64,64,128]{3,2,1,0:T(8,128)(2,1)}, bf16[2,64,64,128]{3,2,1,0:T(8,128)(2,1)S(1)}, u32[]{:S(2)}, u32[]{:S(2)}) collective-permute-start(bf16[2,64,64,128]{3,2,1,0:T(8,128)(2,1)} %bitcast.14), channel_id=1, source_target_pairs={{16,1},{1,17},{18,2},{3,19},{20,4},{5,21},{22,6},{7,23},{24,8},{9,... | collective-permute-start | bytes 6291464 | tf_op jit(solution)/shard_map/ppermute | solution.py:153
  3.9 1.6 %copy-start = (bf16[1,2,64,64,128]{4,3,2,1,0:T(8,128)(2,1)S(1)}, bf16[1,2,64,64,128]{4,3,2,1,0:T(8,128)(2,1)}, u32[]{:S(2)}) copy-start(bf16[1,2,64,64,128]{4,3,2,1,0:T(8,128)(2,1)} %param.4) | copy-start | bytes 6291460
  5.5 0.9 %copy-start.1 = (bf16[64,1024]{1,0:T(8,128)(2,1)S(1)}, bf16[64,1024]{1,0:T(8,128)(2,1)}, u32[]{:S(2)}) copy-start(bf16[64,1024]{1,0:T(8,128)(2,1)} %occ.1) | copy-start | bytes 393220
  6.5 0.7 %copy-start.2 = (bf16[1,64,64]{2,1,0:T(8,128)(2,1)S(1)}, bf16[1,64,64]{2,1,0:T(8,128)(2,1)}, u32[]{:S(2)}) copy-start(bf16[1,64,64]{2,1,0:T(8,128)(2,1)} %virt.1) | copy-start | bytes 24580
  7.2 0.7 %copy-start.3 = (s32[1,2]{1,0:T(1,128)S(1)}, s32[1,2]{1,0:T(1,128)}, u32[]{:S(2)}) copy-start(s32[1,2]{1,0:T(1,128)} %lists.3) | copy-start | bytes 28
  38.1 5.1 %collective-permute-start.1 = (bf16[2,64,64,128]{3,2,1,0:T(8,128)(2,1)S(1)}, bf16[2,64,64,128]{3,2,1,0:T(8,128)(2,1)S(1)}, u32[]{:S(2)}, u32[]{:S(2)}) collective-permute-start(bf16[2,64,64,128]{3,2,1,0:T(8,128)(2,1)S(1)} %collective-permute-done), channel_id=1, source_target_pairs={{1,0}} | collective-permute-start | bytes 6291464 | tf_op jit(solution)/shard_map/ppermute | solution.py:160
  44.0 5.0 %collective-permute-start.2 = (f32[128,128]{1,0:T(8,128)S(1)}, f32[128,128]{1,0:T(8,128)S(1)}, u32[]{:S(2)}, u32[]{:S(2)}) collective-permute-start(f32[128,128]{1,0:T(8,128)S(1)} %shard_map.48), channel_id=1, source_target_pairs={{17,1},{19,3},{21,5},{23,7},{25,9},{27,11},{29,13},{31,15},{33,17}... | collective-permute-start | bytes 196616 | tf_op jit(solution)/shard_map/ppermute | solution.py:163

commit v3 on v2

--- a/solution.py
+++ b/solution.py
@@ -7,7 +7,7 @@
 
 VMEM = pl.BlockSpec(memory_space=pltpu.VMEM)
 SMEM = pl.BlockSpec(memory_space=pltpu.SMEM)
-ANY = pl.BlockSpec(memory_space=pl.ANY)
+HBM = pl.BlockSpec(memory_space=pltpu.HBM)
 LIMIT = 24 * 2**20
 PIECES = 4
 GROUP = 4
@@ -18,13 +18,17 @@
     return lax.rem(lax.axis_index("bas"), 2) == 1
 
 
-def is_first():
-    return jnp.logical_and(lax.axis_index("bas") == 0, lax.axis_index("aux") == 0)
-
-
-def blocks_kernel(lists, occ, virt, slab, sent, upper, spread, held, sem):
-    fetch = pltpu.make_async_copy(slab, held, sem)
-    fetch.start()
+def blocks_kernel(lists_hbm, occ_hbm, virt_hbm, slab, sent, upper, spread, held, lists, occ, virt, sems):
+    fetches = [
+        pltpu.make_async_copy(lists_hbm, lists, sems.at[0]),
+        pltpu.make_async_copy(occ_hbm, occ, sems.at[1]),
+        pltpu.make_async_copy(virt_hbm, virt, sems.at[2]),
+        pltpu.make_async_copy(slab, held, sems.at[3]),
+    ]
+    for fetch in fetches:
+        fetch.start()
+    fetches[0].wait()
+    fetches[1].wait()
     rows, width = occ.shape[0], 2 * occ.shape[0]
     low_lanes = lax.broadcasted_iota(jnp.int32, (rows, width), 1) < rows
 
@@ -38,12 +42,13 @@
         tile = occ[:, t * width : (t + 1) * width].astype(jnp.float32)
         sent[2 * t] = jnp.where(low_lanes, tile, own).astype(sent.dtype)
         sent[2 * t + 1] = jnp.where(low_lanes, pltpu.roll(tile, rows, 1), own).astype(sent.dtype)
+    fetches[2].wait()
     v = virt[0].astype(jnp.float32)
     v = jnp.where(is_odd(), v, v.T)
     zero = jnp.zeros_like(v)
     strips = [jnp.concatenate([v if i == j else zero for j in range(GROUP)], axis=1) for i in range(GROUP)]
     spread[...] = jnp.concatenate(strips, axis=0).astype(spread.dtype)
-    fetch.wait()
+    fetches[3].wait()
 
 
 def blocks_of(lists, occ, virt, slab):
@@ -56,11 +61,16 @@
             jax.ShapeDtypeStruct((GROUP * rows, GROUP * rows), virt.dtype),
             jax.ShapeDtypeStruct(slab.shape, slab.dtype),
         ],
-        in_specs=[SMEM, VMEM, VMEM, ANY],
+        in_specs=[HBM] * 4,
         out_specs=[VMEM] * 4,
-        scratch_shapes=[pltpu.SemaphoreType.DMA],
+        scratch_shapes=[
+            pltpu.SMEM(lists.shape, lists.dtype),
+            pltpu.VMEM(occ.shape, occ.dtype),
+            pltpu.VMEM(virt.shape, virt.dtype),
+            pltpu.SemaphoreType.DMA((4,)),
+        ],
         compiler_params=pltpu.CompilerParams(vmem_limit_bytes=LIMIT),
-    )(lists, occ, virt, slab)
+    )(*[pltpu.with_memory_space_constraint(x, pltpu.HBM) for x in (lists, occ, virt, slab)])
 
 
 def transform_kernel(lists, upper, got, spread, slab, left, same, halves):
@@ -106,29 +116,19 @@
     )(lists, upper, got, spread, slab)
 
 
-def pair_kernel(left, arrived, handed, out, block, sem):
-    @pl.when(is_first())
-    def _():
-        copy = pltpu.make_async_copy(handed, block, sem)
-        copy.start()
-        copy.wait()
-        store_product(out, left, block)
-
-    @pl.when(jnp.logical_not(is_first()))
-    def _():
-        store_product(out, left, arrived)
+def pair_kernel(left, arrived, out):
+    store_product(out, left, arrived)
 
 
-def pair_product(left, arrived, handed):
+def pair_product(left, arrived):
     cols = arrived.shape[1]
     return pl.pallas_call(
         pair_kernel,
         out_shape=jax.ShapeDtypeStruct((cols, cols), jnp.float32),
-        in_specs=[VMEM, VMEM, ANY],
+        in_specs=[VMEM, VMEM],
         out_specs=VMEM,
-        scratch_shapes=[pltpu.VMEM(arrived.shape, arrived.dtype), pltpu.SemaphoreType.DMA],
         compiler_params=pltpu.CompilerParams(vmem_limit_bytes=LIMIT),
-    )(left, arrived, handed)
+    )(left, arrived)
 
 
 def shards(three_centre, occ_green, virt_blocks, row_lists):
@@ -146,8 +146,6 @@
         for c in range(n_bas):
             if c % 2 == 1:
                 route.append((at(a, c), at(a + 1, c)))
-            elif (a, c) == (0, 0):
-                route.append((at(1, 0), at(0, 1)))
             else:
                 route.append((at(a + 1, c), at(a, c)))
     arrived = lax.ppermute(slab, both, route)
@@ -157,8 +155,7 @@
     left, same = transform(row_lists, upper, got, spread, held)
 
     arrived, left, same = lax.optimization_barrier((arrived, left, same))
-    handed = lax.ppermute(arrived, both, [(at(0, 1), at(0, 0))])
-    pair = pair_product(left, arrived.reshape(-1, aux_cols), handed.reshape(-1, aux_cols))
+    pair = pair_product(left, arrived.reshape(-1, aux_cols))
     back = [(at(a + 1, c), at(a, c)) for a in range(n_aux - 1) for c in range(1, n_bas, 2)]
     returned = lax.ppermute(pair, both, back)
     ahead = jnp.where(is_odd(), returned, pair)

time: 60.4 us -> 56.4 us (0.934)
  local copies, waits for them, and re-layouts: 3.87 us -> 0.01 us
  blocking collectives: 35.8 us -> 38.7 us
  waiting for transfers between devices: 7.34 us -> 4.66 us
  starting transfers between devices: 6.65 us -> 5.49 us
  Pallas kernels: 5.76 us -> 6.58 us
    unnamed x8 -> x2, local copies, waits for them, and re-layouts: 3.87 us -> 0.01 us
    ppermute x1 -> x0, waiting for transfers between devices: 3.63 us -> none  [shards(): handed = lax.ppermute(arrived, both, [(at(0, 1), at(0, 0))])]
    all_to_all x1, blocking collectives: 10.5 us -> 13.1 us  [shards(): total = lax.all_to_all(parts, 'bas', 0, 0).sum(axis=0)]
    ppermute x1 -> x0, starting transfers between devices: 1.42 us -> none  [shards(): handed = lax.ppermute(arrived, both, [(at(0, 1), at(0, 0))])]
    ppermute x1, waiting for transfers between devices: 3.71 us -> 4.66 us  [shards(): returned = lax.ppermute(pair, both, back)]
    pallas_call x1, Pallas kernels: 0.91 us -> 1.72 us  [blocks_of(): pl.pallas_call(blocks_kernel, out_shape=[jax.ShapeDtypeStruct((cols // ro...]
  transfers between devices with their start and end apart: 3 -> 2, of which waited for: 2 -> 1; matrix products, arithmetic and copies ran while one was open for 0% -> 0% of each run, Pallas kernels for 8% -> 10%
where the time goes in v3:
time: 56.4 us; the launch traced here: 56.1 us
  blocking collectives  38.7 us (69%)
  Pallas kernels  6.58 us (12%)
  starting transfers between devices  5.49 us (10%)
  waiting for transfers between devices  4.66 us (8%)
  other arithmetic  0.64 us (1%)
    all_to_all x1, blocking collectives, shards(): got = lax.all_to_all(sent, 'bas', 0, 0)  25.6 us
    all_to_all x1, blocking collectives, shards(): total = lax.all_to_all(parts, 'bas', 0, 0).sum(axis=0)  13.1 us
    ppermute x1, waiting for transfers between devices, shards(): returned = lax.ppermute(pair, both, back)  4.66 us
    ppermute x1, starting transfers between devices, shards(): arrived = lax.ppermute(slab, both, route)  4.2 us
    pallas_call x1, Pallas kernels, transform(): pl.pallas_call(transform_kernel, out_shape=[jax.ShapeDtypeStruct((cols, n...  4.09 us
    pallas_call x1, Pallas kernels, blocks_of(): pl.pallas_call(blocks_kernel, out_shape=[jax.ShapeDtypeStruct((cols // ro...  1.72 us
    ppermute x1, starting transfers between devices, shards(): returned = lax.ppermute(pair, both, back)  1.29 us
  transfers between devices with their start and end apart: 2, of which 1 were waited for; matrix products, arithmetic and copies ran while one was open for 0% of the time, Pallas kernels for 10%

profile of v3, /device:TPU:1, one launch (start us, length us, event | category | flops | bytes accessed | tf_op | source)
XLA Modules:
  0.0 56.1 jit_solution(8997656317811688664)
XLA Ops:
  0.0 0.0 copy-start
  0.0 4.2 %collective-permute-start = (bf16[2,64,64,128]{3,2,1,0:T(8,128)(2,1)}, bf16[2,64,64,128]{3,2,1,0:T(8,128)(2,1)S(1)}, u32[]{:S(2)}, u32[]{:S(2)}) collective-permute-start(bf16[2,64,64,128]{3,2,1,0:T(8,128)(2,1)} %bitcast.13), channel_id=1, source_target_pairs={{16,0},{1,17},{18,2},{3,19},{20,4},{5,21},{22,6},{7,23},{24,8},{9,... | collective-permute-start | bytes 6291464 | tf_op jit(solution)/shard_map/ppermute | solution.py:151
  4.2 1.7 %shard_map.46 = (bf16[16,64,128]{2,1,0:T(8,128)(2,1)S(1)}, bf16[64,128]{1,0:T(8,128)(2,1)S(1)}, bf16[256,256]{1,0:T(8,128)(2,1)S(1)}, bf16[128,64,128]{2,1,0:T(8,128)(2,1)S(1)}) custom-call(s32[1,2]{1,0:T(1,128)} %lists.1, bf16[64,1024]{1,0:T(8,128)(2,1)} %occ_hbm.1, bf16[1,64,64]{2,1,0:T(8,128)(2,1)} %virt_hbm.1, bf16[128,64,128]{2,1,0:T(8,128)(2,1)} %bitcast.14), custom_call_target="tpu_custom_call" | custom-call | tf_op jit(solution)/shard_map/pallas_call | solution.py:56
  5.9 25.6 %all_to_all.10.got = bf16[16,64,128]{2,1,0:T(8,128)(2,1)S(1)} all-to-all(bf16[16,64,128]{2,1,0:T(8,128)(2,1)S(1)} %get-tuple-element.15), channel_id=1, replica_groups=mesh['aux'=64,'bas'=16] {'bas'}, dimensions={0} | all-to-all | bytes 524288 | tf_op jit(solution)/shard_map/all_to_all | solution.py:154
  31.6 0.0 copy-done
  31.6 4.1 %shard_map.47 = (bf16[128,8192]{1,0:T(8,128)(2,1)S(1)}, f32[128,128]{1,0:T(8,128)S(1)}) custom-call(s32[1,2]{1,0:T(1,128)S(1)} %copy-done, bf16[64,128]{1,0:T(8,128)(2,1)S(1)} %get-tuple-element.14.upper, bf16[16,64,128]{2,1,0:T(8,128)(2,1)S(1)} %all_to_all.10.got, bf16[256,256]{1,0:T(8,128)(2,1)S(1)} %get-tuple-element.16.spread, ...), custom_call_target="tpu_custom_call" | custom-call | tf_op jit(solution)/shard_map/pallas_call | solution.py:106
  35.7 0.0 collective-permute-done
  35.7 0.8 %shard_map.48 = f32[128,128]{1,0:T(8,128)S(1)} custom-call(bf16[128,8192]{1,0:T(8,128)(2,1)S(1)} %get-tuple-element.21.left, bf16[8192,128]{1,0:T(8,128)(2,1)S(1)} %bitcast.11), custom_call_target="tpu_custom_call" | custom-call | tf_op jit(solution)/shard_map/pallas_call | solution.py:125
  36.5 1.3 %collective-permute-start.1 = (f32[128,128]{1,0:T(8,128)S(1)}, f32[128,128]{1,0:T(8,128)S(1)}, u32[]{:S(2)}, u32[]{:S(2)}) collective-permute-start(f32[128,128]{1,0:T(8,128)S(1)} %shard_map.48), channel_id=1, source_target_pairs={{17,1},{19,3},{21,5},{23,7},{25,9},{27,11},{29,13},{31,15},{33,17}... | collective-permute-start | bytes 196616 | tf_op jit(solution)/shard_map/ppermute | solution.py:160
  37.8 4.7 %collective-permute-done.1 = f32[128,128]{1,0:T(8,128)S(1)} collective-permute-done((f32[128,128]{1,0:T(8,128)S(1)}, f32[128,128]{1,0:T(8,128)S(1)}, u32[]{:S(2)}, u32[]{:S(2)}) %collective-permute-start.1) | collective-permute-done | bytes 65568 | tf_op jit(solution)/shard_map/ppermute | solution.py:160
  42.5 13.1 %all_to_all.11 = f32[16,2,8,128]{3,2,1,0:T(8,128)S(1)} all-to-all(f32[16,2,8,128]{3,2,1,0:T(8,128)S(1)} %pad_maximum_fusion), channel_id=1, replica_groups=mesh['aux'=64,'bas'=16] {'bas'}, dimensions={0} | all-to-all | bytes 262144 | tf_op jit(solution)/shard_map/all_to_all | solution.py:165
  55.5 0.6 %reduce_sum.9 = f32[2,8,128]{2,1,0:T(8,128)} reduce(f32[16,2,8,128]{3,2,1,0:T(8,128)S(1)} %all_to_all.11, f32[]{:T(128)} %constant.11.clone.1), dimensions={0}, to_apply=%region_0.1 | reduce | flops 30720 | bytes 139268 | tf_op jit(solution)/shard_map/reduce_sum | solution.py:165
  (2 shorter events, 0.0 us)
Async XLA Ops:
  0.0 31.6 %copy-start = (s32[1,2]{1,0:T(1,128)S(1)}, s32[1,2]{1,0:T(1,128)}, u32[]{:S(2)}) copy-start(s32[1,2]{1,0:T(1,128)} %lists.1) | copy-start | bytes 28
  0.0 35.7 %collective-permute-start = (bf16[2,64,64,128]{3,2,1,0:T(8,128)(2,1)}, bf16[2,64,64,128]{3,2,1,0:T(8,128)(2,1)S(1)}, u32[]{:S(2)}, u32[]{:S(2)}) collective-permute-start(bf16[2,64,64,128]{3,2,1,0:T(8,128)(2,1)} %bitcast.13), channel_id=1, source_target_pairs={{16,0},{1,17},{18,2},{3,19},{20,4},{5,21},{22,6},{7,23},{24,8},{9,... | collective-permute-start | bytes 6291464 | tf_op jit(solution)/shard_map/ppermute | solution.py:151
  36.5 6.0 %collective-permute-start.1 = (f32[128,128]{1,0:T(8,128)S(1)}, f32[128,128]{1,0:T(8,128)S(1)}, u32[]{:S(2)}, u32[]{:S(2)}) collective-permute-start(f32[128,128]{1,0:T(8,128)S(1)} %shard_map.48), channel_id=1, source_target_pairs={{17,1},{19,3},{21,5},{23,7},{25,9},{27,11},{29,13},{31,15},{33,17}... | collective-permute-start | bytes 196616 | tf_op jit(solution)/shard_map/ppermute | solution.py:160

commit v4 on v3

--- a/solution.py
+++ b/solution.py
@@ -116,19 +116,27 @@
     )(lists, upper, got, spread, slab)
 
 
-def pair_kernel(left, arrived, out):
-    store_product(out, left, arrived)
+def pair_kernel(left, *refs):
+    *arrived, out = refs
+    depth = arrived[0].shape[0]
+    step = depth // 2
+    total = jnp.zeros(out.shape, jnp.float32)
+    for k, block in enumerate(arrived):
+        for i in range(0, depth, step):
+            span = left[:, k * depth + i : k * depth + i + step]
+            total += jnp.dot(span, block[i : i + step], preferred_element_type=jnp.float32)
+    out[...] = jnp.where(is_odd(), total, total.T)
 
 
 def pair_product(left, arrived):
-    cols = arrived.shape[1]
+    cols = arrived[0].shape[1]
     return pl.pallas_call(
         pair_kernel,
         out_shape=jax.ShapeDtypeStruct((cols, cols), jnp.float32),
-        in_specs=[VMEM, VMEM],
+        in_specs=[VMEM] * (1 + len(arrived)),
         out_specs=VMEM,
         compiler_params=pltpu.CompilerParams(vmem_limit_bytes=LIMIT),
-    )(left, arrived)
+    )(left, *arrived)
 
 
 def shards(three_centre, occ_green, virt_blocks, row_lists):
@@ -148,14 +156,14 @@
                 route.append((at(a, c), at(a + 1, c)))
             else:
                 route.append((at(a + 1, c), at(a, c)))
-    arrived = lax.ppermute(slab, both, route)
+    arrived = [lax.ppermute(slab[k], both, route) for k in range(kb)]
 
     sent, upper, spread, held = blocks_of(row_lists, occ_green, virt_blocks, slab.reshape(kb * bb, bb, aux_cols))
     got = lax.all_to_all(sent, "bas", 0, 0)
     left, same = transform(row_lists, upper, got, spread, held)
 
     arrived, left, same = lax.optimization_barrier((arrived, left, same))
-    pair = pair_product(left, arrived.reshape(-1, aux_cols))
+    pair = pair_product(left, [block.reshape(-1, aux_cols) for block in arrived])
     back = [(at(a + 1, c), at(a, c)) for a in range(n_aux - 1) for c in range(1, n_bas, 2)]
     returned = lax.ppermute(pair, both, back)
     ahead = jnp.where(is_odd(), returned, pair)

time: 56.4 us -> 58 us (1.028)
  blocking collectives: 38.7 us -> 35 us
  starting transfers between devices: 5.49 us -> 8.42 us
  local copies, waits for them, and re-layouts: 0.01 us -> 1.72 us
  waiting for transfers between devices: 4.66 us -> 5.24 us
    ppermute x1 -> x2, starting transfers between devices: 4.2 us -> 7.13 us  [shards(): arrived = [lax.ppermute(slab[k], both, route) for k in range(kb)]]
    all_to_all x1, blocking collectives: 13.1 us -> 11.2 us  [shards(): total = lax.all_to_all(parts, 'bas', 0, 0).sum(axis=0)]
    all_to_all x1, blocking collectives: 25.6 us -> 23.9 us  [shards(): got = lax.all_to_all(sent, 'bas', 0, 0)]
    squeeze x0 -> x1, local copies, waits for them, and re-layouts: none -> 1.71 us  [shards(): arrived = [lax.ppermute(slab[k], both, route) for k in range(kb)]]
  transfers between devices with their start and end apart: 2 -> 3, of which waited for: 1 -> 1; matrix products, arithmetic and copies ran while one was open for 0% -> 0% of each run, Pallas kernels for 10% -> 10%
where the time goes in v4:
time: 58 us; the launch traced here: 57.7 us
  blocking collectives  35 us (60%)
  starting transfers between devices  8.42 us (15%)
  Pallas kernels  6.6 us (11%)
  waiting for transfers between devices  5.24 us (9%)
  local copies, waits for them, and re-layouts  1.72 us (3%)
  other arithmetic  0.64 us (1%)
    all_to_all x1, blocking collectives, shards(): got = lax.all_to_all(sent, 'bas', 0, 0)  23.9 us
    all_to_all x1, blocking collectives, shards(): total = lax.all_to_all(parts, 'bas', 0, 0).sum(axis=0)  11.2 us
    ppermute x2, starting transfers between devices, shards(): arrived = [lax.ppermute(slab[k], both, route) for k in range(kb)]  7.13 us
    ppermute x1, waiting for transfers between devices, shards(): returned = lax.ppermute(pair, both, back)  5.24 us
    pallas_call x1, Pallas kernels, transform(): pl.pallas_call(transform_kernel, out_shape=[jax.ShapeDtypeStruct((cols, n...  4.09 us
    pallas_call x1, Pallas kernels, blocks_of(): pl.pallas_call(blocks_kernel, out_shape=[jax.ShapeDtypeStruct((cols // ro...  1.73 us
    squeeze x1, local copies, waits for them, and re-layouts, shards(): arrived = [lax.ppermute(slab[k], both, route) for k in range(kb)]  1.71 us
    ppermute x1, starting transfers between devices, shards(): returned = lax.ppermute(pair, both, back)  1.29 us
  transfers between devices with their start and end apart: 3, of which 1 were waited for; matrix products, arithmetic and copies ran while one was open for 0% of the time, Pallas kernels for 10%

profile of v4, /device:TPU:1, one launch (start us, length us, event | category | flops | bytes accessed | tf_op | source)
XLA Modules:
  0.0 57.7 jit_solution(17569470273779642936)
XLA Ops:
  0.0 1.7 %slice_bitcast_fusion = (bf16[64,64,128]{2,1,0:T(8,128)(2,1)S(1)}, bf16[64,64,128]{2,1,0:T(8,128)(2,1)S(1)}) fusion(bf16[1,2,64,64,128]{4,3,2,1,0:T(8,128)(2,1)} %param.4), kind=kLoop, calls=%fused_computation | loop fusion | bytes 4194304 | tf_op jit(solution)/shard_map/squeeze | solution.py:159
  1.7 0.0 copy-start
  1.7 4.0 %collective-permute-start = (bf16[64,64,128]{2,1,0:T(8,128)(2,1)S(1)}, bf16[64,64,128]{2,1,0:T(8,128)(2,1)S(1)}, u32[]{:S(2)}, u32[]{:S(2)}) collective-permute-start(bf16[64,64,128]{2,1,0:T(8,128)(2,1)S(1)} %get-tuple-element.26), channel_id=1, source_target_pairs={{16,0},{1,17},{18,2},{3,19},{20,4},{5,21},{22,6},{7,23},{24,8},{9,... | collective-permute-start | bytes 3145736 | tf_op jit(solution)/shard_map/ppermute | solution.py:159
  5.7 3.1 %collective-permute-start.1 = (bf16[64,64,128]{2,1,0:T(8,128)(2,1)S(1)}, bf16[64,64,128]{2,1,0:T(8,128)(2,1)S(1)}, u32[]{:S(2)}, u32[]{:S(2)}) collective-permute-start(bf16[64,64,128]{2,1,0:T(8,128)(2,1)S(1)} %get-tuple-element.25), channel_id=1, source_target_pairs={{16,0},{1,17},{18,2},{3,19},{20,4},{5,21},{22,6},{7,23},{24,8},{9,... | collective-permute-start | bytes 3145736 | tf_op jit(solution)/shard_map/ppermute | solution.py:159
  8.9 1.7 %shard_map.46 = (bf16[16,64,128]{2,1,0:T(8,128)(2,1)S(1)}, bf16[64,128]{1,0:T(8,128)(2,1)S(1)}, bf16[256,256]{1,0:T(8,128)(2,1)S(1)}, bf16[128,64,128]{2,1,0:T(8,128)(2,1)S(1)}) custom-call(s32[1,2]{1,0:T(1,128)} %lists.1, bf16[64,1024]{1,0:T(8,128)(2,1)} %occ_hbm.1, bf16[1,64,64]{2,1,0:T(8,128)(2,1)} %virt_hbm.1, bf16[128,64,128]{2,1,0:T(8,128)(2,1)} %bitcast.18), custom_call_target="tpu_custom_call" | custom-call | tf_op jit(solution)/shard_map/pallas_call | solution.py:56
  10.6 23.9 %all_to_all.10.got = bf16[16,64,128]{2,1,0:T(8,128)(2,1)S(1)} all-to-all(bf16[16,64,128]{2,1,0:T(8,128)(2,1)S(1)} %get-tuple-element.16), channel_id=1, replica_groups=mesh['aux'=64,'bas'=16] {'bas'}, dimensions={0} | all-to-all | bytes 524288 | tf_op jit(solution)/shard_map/all_to_all | solution.py:162
  34.5 0.0 copy-done
  34.5 4.1 %shard_map.47 = (bf16[128,8192]{1,0:T(8,128)(2,1)S(1)}, f32[128,128]{1,0:T(8,128)S(1)}) custom-call(s32[1,2]{1,0:T(1,128)S(1)} %copy-done, bf16[64,128]{1,0:T(8,128)(2,1)S(1)} %get-tuple-element.15.upper, bf16[16,64,128]{2,1,0:T(8,128)(2,1)S(1)} %all_to_all.10.got, bf16[256,256]{1,0:T(8,128)(2,1)S(1)} %get-tuple-element.17.spread, ...), custom_call_target="tpu_custom_call" | custom-call | tf_op jit(solution)/shard_map/pallas_call | solution.py:106
  38.6 0.0 collective-permute-done
  38.6 0.0 collective-permute-done.1
  38.6 0.8 %shard_map.48 = f32[128,128]{1,0:T(8,128)S(1)} custom-call(bf16[128,8192]{1,0:T(8,128)(2,1)S(1)} %get-tuple-element.22.left, bf16[4096,128]{1,0:T(8,128)(2,1)S(1)} %bitcast.15, bf16[4096,128]{1,0:T(8,128)(2,1)S(1)} %bitcast.16), custom_call_target="tpu_custom_call" | custom-call | tf_op jit(solution)/shard_map/pallas_call | solution.py:133
  39.4 1.3 %collective-permute-start.2 = (f32[128,128]{1,0:T(8,128)S(1)}, f32[128,128]{1,0:T(8,128)S(1)}, u32[]{:S(2)}, u32[]{:S(2)}) collective-permute-start(f32[128,128]{1,0:T(8,128)S(1)} %shard_map.48), channel_id=1, source_target_pairs={{17,1},{19,3},{21,5},{23,7},{25,9},{27,11},{29,13},{31,15},{33,17}... | collective-permute-start | bytes 196616 | tf_op jit(solution)/shard_map/ppermute | solution.py:168
  40.7 5.2 %collective-permute-done.2 = f32[128,128]{1,0:T(8,128)S(1)} collective-permute-done((f32[128,128]{1,0:T(8,128)S(1)}, f32[128,128]{1,0:T(8,128)S(1)}, u32[]{:S(2)}, u32[]{:S(2)}) %collective-permute-start.2) | collective-permute-done | bytes 65568 | tf_op jit(solution)/shard_map/ppermute | solution.py:168
  46.0 11.2 %all_to_all.11 = f32[16,2,8,128]{3,2,1,0:T(8,128)S(1)} all-to-all(f32[16,2,8,128]{3,2,1,0:T(8,128)S(1)} %pad_maximum_fusion), channel_id=1, replica_groups=mesh['aux'=64,'bas'=16] {'bas'}, dimensions={0} | all-to-all | bytes 262144 | tf_op jit(solution)/shard_map/all_to_all | solution.py:173
  57.1 0.6 %reduce_sum.9 = f32[2,8,128]{2,1,0:T(8,128)} reduce(f32[16,2,8,128]{3,2,1,0:T(8,128)S(1)} %all_to_all.11, f32[]{:T(128)} %constant.11.clone.1), dimensions={0}, to_apply=%region_0.1 | reduce | flops 30720 | bytes 139268 | tf_op jit(solution)/shard_map/reduce_sum | solution.py:173
  (2 shorter events, 0.0 us)
Async XLA Ops:
  1.7 32.8 %copy-start = (s32[1,2]{1,0:T(1,128)S(1)}, s32[1,2]{1,0:T(1,128)}, u32[]{:S(2)}) copy-start(s32[1,2]{1,0:T(1,128)} %lists.1) | copy-start | bytes 28
  1.7 36.9 %collective-permute-start = (bf16[64,64,128]{2,1,0:T(8,128)(2,1)S(1)}, bf16[64,64,128]{2,1,0:T(8,128)(2,1)S(1)}, u32[]{:S(2)}, u32[]{:S(2)}) collective-permute-start(bf16[64,64,128]{2,1,0:T(8,128)(2,1)S(1)} %get-tuple-element.26), channel_id=1, source_target_pairs={{16,0},{1,17},{18,2},{3,19},{20,4},{5,21},{22,6},{7,23},{24,8},{9,... | collective-permute-start | bytes 3145736 | tf_op jit(solution)/shard_map/ppermute | solution.py:159
  5.7 32.9 %collective-permute-start.1 = (bf16[64,64,128]{2,1,0:T(8,128)(2,1)S(1)}, bf16[64,64,128]{2,1,0:T(8,128)(2,1)S(1)}, u32[]{:S(2)}, u32[]{:S(2)}) collective-permute-start(bf16[64,64,128]{2,1,0:T(8,128)(2,1)S(1)} %get-tuple-element.25), channel_id=1, source_target_pairs={{16,0},{1,17},{18,2},{3,19},{20,4},{5,21},{22,6},{7,23},{24,8},{9,... | collective-permute-start | bytes 3145736 | tf_op jit(solution)/shard_map/ppermute | solution.py:159
  39.4 6.5 %collective-permute-start.2 = (f32[128,128]{1,0:T(8,128)S(1)}, f32[128,128]{1,0:T(8,128)S(1)}, u32[]{:S(2)}, u32[]{:S(2)}) collective-permute-start(f32[128,128]{1,0:T(8,128)S(1)} %shard_map.48), channel_id=1, source_target_pairs={{17,1},{19,3},{21,5},{23,7},{25,9},{27,11},{29,13},{31,15},{33,17}... | collective-permute-start | bytes 196616 | tf_op jit(solution)/shard_map/ppermute | solution.py:168

commit v5 on v3

--- a/solution.py
+++ b/solution.py
@@ -162,7 +162,8 @@
 
     cut = aux_cols // n_bas
     parts = jnp.stack([same.reshape(n_bas, cut, aux_cols), ahead.reshape(n_bas, cut, aux_cols)], axis=1)
-    total = lax.all_to_all(parts, "bas", 0, 0).sum(axis=0)
+    parts = parts.reshape(n_bas, 2 * cut, aux_cols).astype(jnp.bfloat16)
+    total = lax.all_to_all(parts, "bas", 0, 0).astype(jnp.float32).sum(axis=0).reshape(2, cut, aux_cols)
     return total.transpose(2, 0, 1)
 
 

time: 56.4 us -> 57.6 us (1.021)
  blocking collectives: 38.7 us -> 9.97 us
  starting transfers between devices: 5.49 us -> 20.2 us
  waiting for transfers between devices: 4.66 us -> 16.1 us
  local copies, waits for them, and re-layouts: 0.01 us -> 2.94 us
  Pallas kernels: 6.58 us -> 7.3 us
    all_to_all x2 -> x1, blocking collectives: 38.7 us -> 9.97 us  [shards(): lax.all_to_all(parts, 'bas', 0, 0).astype(jnp.float32).sum(axis=0)]
    all_to_all x0 -> x1, starting transfers between devices: none -> 14.7 us  [shards(): got = lax.all_to_all(sent, 'bas', 0, 0)]
    all_to_all x0 -> x1, waiting for transfers between devices: none -> 11.9 us  [shards(): got = lax.all_to_all(sent, 'bas', 0, 0)]
    unnamed x2 -> x6, local copies, waits for them, and re-layouts: 0.01 us -> 2.94 us
    pallas_call x1, Pallas kernels: 1.72 us -> 2.42 us  [blocks_of(): pl.pallas_call(blocks_kernel, out_shape=[jax.ShapeDtypeStruct((cols // ro...]
  transfers between devices with their start and end apart: 2 -> 3, of which waited for: 1 -> 2; matrix products, arithmetic and copies ran while one was open for 0% -> 0% of each run, Pallas kernels for 10% -> 11%
where the time goes in v5:
time: 57.6 us; the launch traced here: 57.2 us
  starting transfers between devices  20.2 us (35%)
  waiting for transfers between devices  16.1 us (28%)
  blocking collectives  9.97 us (17%)
  Pallas kernels  7.3 us (13%)
  local copies, waits for them, and re-layouts  2.94 us (5%)
  other arithmetic  0.66 us (1%)
    all_to_all x1, starting transfers between devices, shards(): got = lax.all_to_all(sent, 'bas', 0, 0)  14.7 us
    all_to_all x1, waiting for transfers between devices, shards(): got = lax.all_to_all(sent, 'bas', 0, 0)  11.9 us
    all_to_all x1, blocking collectives, shards(): lax.all_to_all(parts, 'bas', 0, 0).astype(jnp.float32).sum(axis=0)  9.97 us
    ppermute x1, waiting for transfers between devices, shards(): returned = lax.ppermute(pair, both, back)  4.25 us
    ppermute x1, starting transfers between devices, shards(): arrived = lax.ppermute(slab, both, route)  4.2 us
    pallas_call x1, Pallas kernels, transform(): pl.pallas_call(transform_kernel, out_shape=[jax.ShapeDtypeStruct((cols, n...  4.09 us
    unnamed x6, local copies, waits for them, and re-layouts  2.94 us
    pallas_call x1, Pallas kernels, blocks_of(): pl.pallas_call(blocks_kernel, out_shape=[jax.ShapeDtypeStruct((cols // ro...  2.42 us
  transfers between devices with their start and end apart: 3, of which 2 were waited for; matrix products, arithmetic and copies ran while one was open for 0% of the time, Pallas kernels for 11%

profile of v5, /device:TPU:1, one launch (start us, length us, event | category | flops | bytes accessed | tf_op | source)
XLA Modules:
  0.0 57.2 jit_solution(9963890628273461124)
XLA Ops:
  0.0 0.0 copy-start.2
  0.0 4.2 %collective-permute-start = (bf16[2,64,64,128]{3,2,1,0:T(8,128)(2,1)}, bf16[2,64,64,128]{3,2,1,0:T(8,128)(2,1)S(1)}, u32[]{:S(2)}, u32[]{:S(2)}) collective-permute-start(bf16[2,64,64,128]{3,2,1,0:T(8,128)(2,1)} %bitcast.17), channel_id=1, source_target_pairs={{16,0},{1,17},{18,2},{3,19},{20,4},{5,21},{22,6},{7,23},{24,8},{9,... | collective-permute-start | bytes 6291464 | tf_op jit(solution)/shard_map/ppermute | solution.py:151
  4.2 2.4 %shard_map.46 = (bf16[16,64,128]{2,1,0:T(8,128)(2,1)}, bf16[64,128]{1,0:T(8,128)(2,1)S(1)}, bf16[256,256]{1,0:T(8,128)(2,1)S(1)}, bf16[128,64,128]{2,1,0:T(8,128)(2,1)S(1)}) custom-call(s32[1,2]{1,0:T(1,128)} %lists.1, bf16[64,1024]{1,0:T(8,128)(2,1)} %occ_hbm.1, bf16[1,64,64]{2,1,0:T(8,128)(2,1)} %virt_hbm.1, bf16[128,64,128]{2,1,0:T(8,128)(2,1)} %bitcast.18), custom_call_target="tpu_custom_call" | custom-call | tf_op jit(solution)/shard_map/pallas_call | solution.py:56
  6.6 0.0 copy-start
  6.6 1.3 %copy-done = bf16[128,64,128]{2,1,0:T(8,128)(2,1)} copy-done((bf16[128,64,128]{2,1,0:T(8,128)(2,1)}, bf16[128,64,128]{2,1,0:T(8,128)(2,1)S(1)}, u32[]{:S(2)}) %copy-start) | copy-done | bytes 2097176
  8.0 14.7 %all-to-all-start = ((bf16[16,64,128]{2,1,0:T(8,128)(2,1)}), bf16[16,64,128]{2,1,0:T(8,128)(2,1)S(1)}, u32[]{:S(2)}, u32[]{:S(2)}) async-start(bf16[16,64,128]{2,1,0:T(8,128)(2,1)} %get-tuple-element.15), calls=%async_computation | async-start | bytes 524288 | tf_op jit(solution)/shard_map/all_to_all | solution.py:154
  22.7 11.9 %all-to-all-done.got = bf16[16,64,128]{2,1,0:T(8,128)(2,1)S(1)} async-done(((bf16[16,64,128]{2,1,0:T(8,128)(2,1)}), bf16[16,64,128]{2,1,0:T(8,128)(2,1)S(1)}, u32[]{:S(2)}, u32[]{:S(2)}) %all-to-all-start) | async-done | bytes 262176 | tf_op jit(solution)/shard_map/all_to_all | solution.py:154
  34.5 0.0 copy-done.2
  34.5 0.0 copy-start.1
  34.5 1.6 %copy-done.1 = bf16[128,64,128]{2,1,0:T(8,128)(2,1)S(1)} copy-done((bf16[128,64,128]{2,1,0:T(8,128)(2,1)S(1)}, bf16[128,64,128]{2,1,0:T(8,128)(2,1)}, u32[]{:S(2)}) %copy-start.1) | copy-done | bytes 2097176
  36.1 4.1 %shard_map.47 = (bf16[128,8192]{1,0:T(8,128)(2,1)S(1)}, f32[128,128]{1,0:T(8,128)S(1)}) custom-call(s32[1,2]{1,0:T(1,128)S(1)} %copy-done.2, bf16[64,128]{1,0:T(8,128)(2,1)S(1)} %get-tuple-element.14.upper, bf16[16,64,128]{2,1,0:T(8,128)(2,1)S(1)} %all-to-all-done.got, bf16[256,256]{1,0:T(8,128)(2,1)S(1)} %get-tuple-element.16.spread, ...), custom_call_target="tpu_custom_call" | custom-call | tf_op jit(solution)/shard_map/pallas_call | solution.py:106
  40.2 0.0 collective-permute-done
  40.2 0.8 %shard_map.48 = f32[128,128]{1,0:T(8,128)S(1)} custom-call(bf16[128,8192]{1,0:T(8,128)(2,1)S(1)} %get-tuple-element.21.left, bf16[8192,128]{1,0:T(8,128)(2,1)S(1)} %bitcast.16), custom_call_target="tpu_custom_call" | custom-call | tf_op jit(solution)/shard_map/pallas_call | solution.py:125
  41.0 1.3 %collective-permute-start.1 = (bf16[128,128]{1,0:T(8,128)(2,1)S(1)}, bf16[128,128]{1,0:T(8,128)(2,1)S(1)}, u32[]{:S(2)}, u32[]{:S(2)}) collective-permute-start(bf16[128,128]{1,0:T(8,128)(2,1)S(1)} %convert.14), channel_id=1, source_target_pairs={{17,1},{19,3},{21,5},{23,7},{25,9},{27,11},{29,13},{31,15},{33,17}... | collective-permute-start | bytes 98312 | tf_op jit(solution)/shard_map/ppermute | solution.py:160
  42.4 4.3 %collective-permute-done.1 = bf16[128,128]{1,0:T(8,128)(2,1)S(1)} collective-permute-done((bf16[128,128]{1,0:T(8,128)(2,1)S(1)}, bf16[128,128]{1,0:T(8,128)(2,1)S(1)}, u32[]{:S(2)}, u32[]{:S(2)}) %collective-permute-start.1) | collective-permute-done | bytes 32800 | tf_op jit(solution)/shard_map/ppermute | solution.py:160
  46.7 10.0 %all_to_all.10 = bf16[16,16,128]{2,1,0:T(8,128)(2,1)S(1)} all-to-all(bf16[16,16,128]{2,1,0:T(8,128)(2,1)S(1)} %maximum_bitcast_fusion), channel_id=1, replica_groups=mesh['aux'=64,'bas'=16] {'bas'}, dimensions={0} | all-to-all | bytes 131072 | tf_op jit(solution)/shard_map/all_to_all | solution.py:166
  56.6 0.6 %convert_reduce_fusion = f32[16,128]{1,0:T(8,128)} fusion(bf16[16,16,128]{2,1,0:T(8,128)(2,1)S(1)} %all_to_all.10), kind=kLoop, calls=%fused_computation | loop fusion | flops 63488 | bytes 73728 | tf_op jit(solution)/shard_map/reduce_sum | solution.py:166
  (4 shorter events, 0.0 us)
Async XLA Ops:
  0.0 34.5 %copy-start.2 = (s32[1,2]{1,0:T(1,128)S(1)}, s32[1,2]{1,0:T(1,128)}, u32[]{:S(2)}) copy-start(s32[1,2]{1,0:T(1,128)} %lists.1) | copy-start | bytes 28
  0.0 40.2 %collective-permute-start = (bf16[2,64,64,128]{3,2,1,0:T(8,128)(2,1)}, bf16[2,64,64,128]{3,2,1,0:T(8,128)(2,1)S(1)}, u32[]{:S(2)}, u32[]{:S(2)}) collective-permute-start(bf16[2,64,64,128]{3,2,1,0:T(8,128)(2,1)} %bitcast.17), channel_id=1, source_target_pairs={{16,0},{1,17},{18,2},{3,19},{20,4},{5,21},{22,6},{7,23},{24,8},{9,... | collective-permute-start | bytes 6291464 | tf_op jit(solution)/shard_map/ppermute | solution.py:151
  6.6 1.4 %copy-start = (bf16[128,64,128]{2,1,0:T(8,128)(2,1)}, bf16[128,64,128]{2,1,0:T(8,128)(2,1)S(1)}, u32[]{:S(2)}) copy-start(bf16[128,64,128]{2,1,0:T(8,128)(2,1)S(1)} %get-tuple-element.17.slab) | copy-start | bytes 6291460
  8.0 26.5 %all-to-all-start = ((bf16[16,64,128]{2,1,0:T(8,128)(2,1)}), bf16[16,64,128]{2,1,0:T(8,128)(2,1)S(1)}, u32[]{:S(2)}, u32[]{:S(2)}) async-start(bf16[16,64,128]{2,1,0:T(8,128)(2,1)} %get-tuple-element.15), calls=%async_computation | async-start | bytes 524288 | tf_op jit(solution)/shard_map/all_to_all | solution.py:154
  34.5 1.6 %copy-start.1 = (bf16[128,64,128]{2,1,0:T(8,128)(2,1)S(1)}, bf16[128,64,128]{2,1,0:T(8,128)(2,1)}, u32[]{:S(2)}) copy-start(bf16[128,64,128]{2,1,0:T(8,128)(2,1)} %copy-done) | copy-start | bytes 6291460
  41.0 5.6 %collective-permute-start.1 = (bf16[128,128]{1,0:T(8,128)(2,1)S(1)}, bf16[128,128]{1,0:T(8,128)(2,1)S(1)}, u32[]{:S(2)}, u32[]{:S(2)}) collective-permute-start(bf16[128,128]{1,0:T(8,128)(2,1)S(1)} %convert.14), channel_id=1, source_target_pairs={{17,1},{19,3},{21,5},{23,7},{25,9},{27,11},{29,13},{31,15},{33,17}... | collective-permute-start | bytes 98312 | tf_op jit(solution)/shard_map/ppermute | solution.py:160
